TPU v7x, 256 devices: a whole 4x4x8 slice. The times are simulated.
256 devices in a mesh: row: 16 (over y, x), col: 16 (over z, core).
Axes of the slice: x: 4, y: 4, z: 8, core: 2. Of those that a mesh axis runs over, the one named last changes fastest.
Arguments:
- ancestor_inverse: float32 [16384, 16384], P('row', 'col'), may hold values from -18 to 18, as said below
- panel: float32 [16384, 1024], P(('row', 'col')), may hold values from -0.046875 to 0.046875
- diag_inverse: float32 [1024, 1024], replicated, may hold values from -0.1875 to 0.1875
- inverse_pattern: int32 [64, 64], replicated, may hold values from 0 to 1, as said below
- panel_pattern: int32 [64, 4], replicated, may hold values 0 or 1
Outputs:
- sigma_panel: float32 [16384, 1024], P(('row', 'col'))
- sigma_diag: float32 [1024, 1024], replicated
Inputs may be any that keep to these rules, and one draw needn't show every extreme that they name: `ancestor_inverse`: symmetric, so entry (i, j) equals entry (j, i). `inverse_pattern`: 1 marks a kept tile; the pattern is symmetric and every diagonal tile is kept. `panel_pattern`: 1 marks a nonzero tile.
All inputs are finite; a program needn't handle non-finite values.
Results may differ from a plain program's by a relative error of at most 0.000075.
Values sent between devices are 32-bit elements; how exact they have to be, the bound alone decides.
No kernel may reach another device: no remote copies, remote signals or barrier semaphores. Data moves between devices by JAX's collectives and lax.ppermute only.
A program may use at most 128 MiB of HBM per device.

v0:
```python
import jax
import jax.numpy as jnp
from jax import lax
from jax.sharding import PartitionSpec as P

TILE = 256


HIGH = lax.Precision.HIGHEST


def from_root(value, axis, source):
    kept = jnp.where(lax.axis_index(axis) == source, value, 0).astype(value.dtype)
    return lax.psum(kept, axis)


def shards(ancestor_inverse, panel, diag_inverse, inverse_pattern, panel_pattern):
    rows_count = lax.axis_size("row")
    cols_count = lax.axis_size("col")
    row_at = lax.axis_index("row")
    col_at = lax.axis_index("col")
    block_rows, block_cols = ancestor_inverse.shape
    piece_rows, panel_width = panel.shape
    inv_factor = jnp.tril(diag_inverse) + jnp.eye(panel_width, dtype=jnp.float32)
    first_row = (row_at * cols_count + col_at) * piece_rows
    tile_ids = (first_row + jnp.arange(piece_rows, dtype=jnp.int32)) // TILE
    one_hot = (
        tile_ids[:, None] == jnp.arange(panel_pattern.shape[0], dtype=jnp.int32)[None, :]
    ).astype(jnp.float32)
    row_flags = jnp.dot(one_hot, panel_pattern.astype(jnp.float32), precision=HIGH)
    local_scaled = jnp.dot(panel * jnp.repeat(row_flags, TILE, axis=1), inv_factor, precision=HIGH)
    row_band = lax.all_gather(local_scaled, "col", axis=0, tiled=True)
    col_ratio = cols_count // rows_count
    root_row = col_at // col_ratio
    broadcast_band = from_root(row_band, "row", root_row)
    row_tiles = block_rows // TILE
    col_tiles = block_cols // TILE
    tile_flags = lax.dynamic_slice(
        inverse_pattern, (row_at * row_tiles, col_at * col_tiles), (row_tiles, col_tiles)
    )
    flag_values = tile_flags.astype(jnp.float32)
    masked_inverse = (
        ancestor_inverse.reshape(row_tiles, TILE, col_tiles, TILE) * flag_values[:, None, :, None]
    ).reshape(block_rows, block_cols)
    sigma_panel = lax.psum_scatter(
        -jnp.dot(masked_inverse, broadcast_band, precision=HIGH),
        "col",
        scatter_dimension=0,
        tiled=True,
    )
    quad_form = jnp.einsum("rj,rk->jk", local_scaled, sigma_panel, precision=HIGH)
    base_term = jnp.einsum("kj,kl->jl", inv_factor, inv_factor, precision=HIGH)
    local_term = -quad_form
    summed_term = lax.psum(local_term, ("row", "col"))
    sigma_diag = base_term + summed_term
    return (sigma_panel, sigma_diag)


def solution(mesh):
    return jax.shard_map(
        shards,
        mesh=mesh,
        in_specs=(P("row", "col"), P(("row", "col"), None), P(), P(), P()),
        out_specs=(P(("row", "col"), None), P()),
        check_vma=False,
    )
```

profile of v0, /device:TPU:1, one launch (start us, length us, event | category | flops | bytes accessed | tf_op | source)
XLA Modules:
  0.0 554.8 jit_solution(3773878319709531673)
XLA Ops:
  7.2 0.0 all-gather.2.cloned.1.call-start
  7.2 0.9 fusion.11
  8.1 0.1 broadcast_in_dim.12
  8.3 4.8 fusion.3
  13.1 0.0 all-gather.2.cloned.1.call-update
  13.1 0.0 all-reduce.3.cloned.1.call-start
  13.2 46.4 %all-gather.2.cloned.1.call-done = f32[1024,1024]{1,0:T(8,128)} async-done(((f32[64,1024]{1,0:T(8,128)}), f32[1024,1024]{1,0:T(8,128)}) %all-gather.2.cloned.1.call-update) | async-done | bytes 4194320 | tf_op jit(solution)/shard_map/all_gather | solution.py:32
  59.6 2.8 broadcast_select_fusion
  62.4 0.0 all-reduce.3.cloned.1.call-update
  62.5 0.0 reduce-scatter.2.cloned.1.call-start
  62.5 0.8 dynamic-slice_convert_fusion
  63.3 0.6 mul.28
  63.9 3.0 copy.9
  66.9 109.3 %all-reduce.3.cloned.1.call-done = f32[1024,1024]{1,0:T(8,128)} async-done(((f32[1024,1024]{1,0:T(8,128)}), f32[1024,1024]{1,0:T(8,128)}) %all-reduce.3.cloned.1.call-update) | async-done | bytes 4194320 | tf_op jit(solution)/shard_map/psum | solution.py:14
  176.1 18.5 %fusion.4 = f32[1024,1024]{1,0:T(8,128)} fusion(f32[1024,1024]{1,0:T(8,128)} %all-reduce.3.cloned.1.call-done, f32[1024,1024]{1,0:T(8,128)} %param.5, f32[1024,1024]{1,0:T(8,128)} %bitcast.9), kind=kOutput, calls=%fused_computation.8 | convolution fusion | flops 12886999040 | bytes 16777216 | tf_op jit(solution)/shard_map/dot_general | solution.py:46
  194.7 0.0 copy-start
  194.7 0.0 reduce-scatter.2.cloned.1.call-update
  194.7 0.2 all-reduce.5.cloned.1.call-start
  194.9 59.5 %reduce-scatter.2.cloned.1.call-done = f32[64,1024]{1,0:T(8,128)} async-done(((f32[1024,1024]{1,0:T(8,128)}), f32[64,1024]{1,0:T(8,128)}) %reduce-scatter.2.cloned.1.call-update) | async-done | bytes 262160 | tf_op jit(solution)/shard_map/reduce_scatter | solution.py:45
  254.4 0.0 copy-done
  254.4 6.0 %convolution_negate_fusion = f32[1024,1024]{1,0:T(8,128)} fusion(f32[64,1024]{1,0:T(8,128)S(1)} %copy-done, f32[64,1024]{1,0:T(8,128)} %reduce-scatter.2.cloned.1.call-done), kind=kOutput, calls=%fused_computation.7 | convolution fusion | flops 806354944 | bytes 4718592 | tf_op jit(solution)/shard_map/rj,rk->jk/dot_general | solution.py:51
  260.4 0.0 all-reduce.5.cloned.1.call-update
  260.4 268.8 %all-reduce.5.cloned.1.call-done = f32[1024,1024]{1,0:T(8,128)} async-done(((f32[1024,1024]{1,0:T(8,128)}), f32[1024,1024]{1,0:T(8,128)}) %all-reduce.5.cloned.1.call-update) | async-done | bytes 4194320 | tf_op jit(solution)/shard_map/psum | solution.py:54
  529.2 19.1 %fusion.9 = f32[1024,1024]{1,0:T(8,128)} fusion(f32[1024,1024]{1,0:T(8,128)} %all-reduce.5.cloned.1.call-done, f32[1024,1024]{1,0:T(8,128)} %param.7), kind=kOutput, calls=%fused_computation.12 | convolution fusion | flops 12891193344 | bytes 12582912 | tf_op jit(solution)/shard_map/kj,kl->jl/dot_general | solution.py:52
  (2 shorter events, 0.1 us)
Async XLA Ops:
  7.2 52.4 %all-gather.2.cloned.1.call-start = ((), (), s32[]{:S(2)}) async-start(), calls=%async_computation.1 | async-start | bytes 4456448 | tf_op jit(solution)/shard_map/all_gather | solution.py:32
  13.1 163.0 %all-reduce.3.cloned.1.call-start = ((), (), s32[]{:S(2)}) async-start(), calls=%async_computation.2 | async-start | bytes 8388608 | tf_op jit(solution)/shard_map/psum | solution.py:14
  62.5 192.0 %reduce-scatter.2.cloned.1.call-start = ((), (), s32[]{:S(2)}) async-start(), calls=%async_computation.3 | async-start | bytes 4456448 | tf_op jit(solution)/shard_map/reduce_scatter | solution.py:45
  194.7 59.8 %copy-start = (f32[64,1024]{1,0:T(8,128)S(1)}, f32[64,1024]{1,0:T(8,128)}, u32[]{:S(2)}) copy-start(f32[64,1024]{1,0:T(8,128)} %fusion.3) | copy-start | bytes 786436
  194.7 334.5 %all-reduce.5.cloned.1.call-start = ((), (), s32[]{:S(2)}) async-start(), calls=%async_computation.4 | async-start | bytes 8388608 | tf_op jit(solution)/shard_map/psum | solution.py:54
Sparse Core Ops, SparseCore 0:
  13.2 46.3 all-gather.1
  63.5 112.5 all-reduce.2
  194.8 59.5 reduce-scatter.1
  260.5 268.5 all-reduce.4
where the time goes:
time: 556 us; the launch traced here: 555 us
  waiting for transfers between devices  484 us (87%)
  matrix products  49.2 us (9%)
  between operations  13.8 us (2%)
    psum x1, waiting for transfers between devices, shards(): summed_term = lax.psum(local_term, ('row', 'col'))  269 us
    psum x1, waiting for transfers between devices, from_root(): return lax.psum(kept, axis)  109 us
    reduce_scatter x1, waiting for transfers between devices, shards(): lax.psum_scatter(-jnp.dot(masked_inverse, broadcast_band, precision=HIGH)...  59.5 us
    all_gather x1, waiting for transfers between devices, shards(): row_band = lax.all_gather(local_scaled, 'col', axis=0, tiled=True)  46.4 us
    dot_general x1, matrix products, shards(): base_term = jnp.einsum('kj,kl->jl', inv_factor, inv_factor, precision=HIGH)  19.1 us
    dot_general x1, matrix products, shards(): jnp.dot(masked_inverse, broadcast_band, precision=HIGH)  18.5 us
  transfers between devices with their start and end apart: 4, of which 4 were waited for; matrix products, arithmetic and copies ran while one was open for 1% of the time, Pallas kernels for 0%

commit v1 on v0

v1 whole, which is shorter than its diff:
```python
import jax
import jax.numpy as jnp
from jax import lax
from jax.sharding import PartitionSpec as P

TILE = 256
HIGH = lax.Precision.HIGH


def z_shift(cols_count, step):
    chips = cols_count // 2
    return [(z * 2 + k, ((z + step) % chips) * 2 + k) for z in range(chips) for k in range(2)]


def gather_col(piece, cols_count):
    chips = cols_count // 2
    col_at = lax.axis_index("col")
    z_at = col_at // 2
    held = jnp.zeros((chips,) + piece.shape, piece.dtype)
    held = lax.dynamic_update_slice(held, piece[None], (z_at, 0, 0))
    up = down = piece
    for step in range(1, chips // 2 + 1):
        up = lax.ppermute(up, "col", z_shift(cols_count, 1))
        held = lax.dynamic_update_slice(held, up[None], ((z_at - step) % chips, 0, 0))
        if step < chips // 2:
            down = lax.ppermute(down, "col", z_shift(cols_count, -1))
            held = lax.dynamic_update_slice(held, down[None], ((z_at + step) % chips, 0, 0))
    other = lax.ppermute(held, "col", [(i, i ^ 1) for i in range(cols_count)])
    first = col_at % 2 == 0
    both = jnp.stack([jnp.where(first, held, other), jnp.where(first, other, held)], axis=1)
    return both.reshape((cols_count * piece.shape[0],) + piece.shape[1:])


def shards(ancestor_inverse, panel, diag_inverse, inverse_pattern, panel_pattern):
    rows_count = lax.axis_size("row")
    cols_count = lax.axis_size("col")
    row_at = lax.axis_index("row")
    col_at = lax.axis_index("col")
    block_rows, block_cols = ancestor_inverse.shape
    piece_rows, width = panel.shape
    inv_factor = jnp.tril(diag_inverse) + jnp.eye(width, dtype=jnp.float32)

    with jax.named_scope("local_scaled"):
        first_row = (row_at * cols_count + col_at) * piece_rows
        flags = lax.dynamic_slice(panel_pattern, (first_row // TILE, 0), (1, width // TILE))
        masked = panel * jnp.repeat(flags.astype(jnp.float32), TILE, axis=1)
        scaled = jnp.dot(masked, inv_factor, precision=HIGH)
    with jax.named_scope("gather_scaled"):
        band = gather_col(scaled, cols_count)
    with jax.named_scope("mask_inverse"):
        row_tiles = block_rows // TILE
        col_tiles = block_cols // TILE
        tile_flags = lax.dynamic_slice(
            inverse_pattern, (row_at * row_tiles, col_at * col_tiles), (row_tiles, col_tiles)
        ).astype(jnp.float32)
        masked_inverse = ancestor_inverse * jnp.repeat(jnp.repeat(tile_flags, TILE, axis=0), TILE, axis=1)
    with jax.named_scope("product"):
        partial = -lax.dot_general(band, masked_inverse, (((0,), (0,)), ((), ())), precision=HIGH)
    with jax.named_scope("sum_row"):
        slice_rows = width // rows_count
        partial = partial.reshape(rows_count, slice_rows, block_cols)
        sigma_t = jnp.sum(lax.all_to_all(partial, "row", 0, 0), axis=0)
    with jax.named_scope("transpose_devices"):
        perm = [(r * cols_count + c, c * cols_count + r) for r in range(rows_count) for c in range(cols_count)]
        sigma_t = lax.ppermute(sigma_t, ("row", "col"), perm)
    with jax.named_scope("quad"):
        quad = jnp.dot(sigma_t, band, precision=HIGH)
        factor_rows = lax.dynamic_slice(inv_factor, (row_at * slice_rows, 0), (slice_rows, width))
        factor_tile = lax.dynamic_slice(factor_rows, (0, col_at * slice_rows), (slice_rows, slice_rows))
        base = lax.dot_general(factor_tile, factor_rows, (((0,), (0,)), ((), ())), precision=HIGH)
        term = base - quad
    with jax.named_scope("sum_diag"):
        term = term.reshape(rows_count, slice_rows // rows_count, width)
        own = jnp.sum(lax.all_to_all(term, "row", 0, 0), axis=0)
        rows = lax.all_to_all(jnp.broadcast_to(own[None], term.shape), "row", 0, 0).reshape(slice_rows, width)
        sigma_diag = gather_col(rows, cols_count)
    with jax.named_scope("sigma_out"):
        pieces = sigma_t.reshape(slice_rows, cols_count, piece_rows).transpose(1, 0, 2)
        pieces = lax.all_to_all(pieces, "col", 0, 0)
        sigma_panel = pieces.reshape(width, piece_rows).T
    return sigma_panel, sigma_diag


def solution(mesh):
    return jax.shard_map(
        shards,
        mesh=mesh,
        in_specs=(P("row", "col"), P(("row", "col"), None), P(), P(), P()),
        out_specs=(P(("row", "col"), None), P()),
        check_vma=False,
    )
```

time: 556 us -> 242 us (0.44)
  waiting for transfers between devices: 484 us -> 52.4 us
  blocking collectives: 0 us -> 109 us
  starting transfers between devices: 0.35 us -> 36.8 us
  matrix products: 49.2 us -> 15.5 us
  between operations: 13.8 us -> 1.01 us
  other arithmetic: 3.62 us -> 15.3 us
  local copies, waits for them, and re-layouts: 3.76 us -> 11.4 us
    psum x2 -> x0, waiting for transfers between devices: 378 us -> none  [the longest x1 269 us: shards(): summed_term = lax.psum(local_term, ('row', 'col'))]
    all_to_all x0 -> x4, blocking collectives: none -> 109 us  [the longest x1 56.7 us: shards(): sigma_t = jnp.sum(lax.all_to_all(partial, 'row', 0, 0), axis=0)]
    reduce_scatter x1 -> x0, waiting for transfers between devices: 59.5 us -> none  [shards(): lax.psum_scatter(-jnp.dot(masked_inverse, broadcast_band, precision=HIGH)...]
    ppermute x0 -> x17, waiting for transfers between devices: none -> 52.4 us  [the longest x8 42.8 us: gather_col(): up = lax.ppermute(up, 'col', z_shift(cols_count, 1))]
    all_gather x1 -> x0, waiting for transfers between devices: 46.4 us -> none  [shards(): row_band = lax.all_gather(local_scaled, 'col', axis=0, tiled=True)]
    ppermute x0 -> x17, starting transfers between devices: none -> 36.8 us  [the longest x6 17.7 us: gather_col(): down = lax.ppermute(down, 'col', z_shift(cols_count, -1))]
    dot_general x5 -> x4, matrix products: 49.2 us -> 15.5 us  [the longest x1 7.27 us: shards(): lax.dot_general(band, masked_inverse, (((0,), (0,)), ((), ())), precision...]
  transfers between devices with their start and end apart: 4 -> 17, of which waited for: 4 -> 10; matrix products, arithmetic and copies ran while one was open for 1% -> 6% of each run, Pallas kernels for 0% -> 0%
where the time goes in v1:
time: 242 us; the launch traced here: 241 us
  blocking collectives  109 us (45%)
  waiting for transfers between devices  52.4 us (22%)
  starting transfers between devices  36.8 us (15%)
  matrix products  15.5 us (6%)
  other arithmetic  15.3 us (6%)
  local copies, waits for them, and re-layouts  11.4 us (5%)
    all_to_all x1, blocking collectives, shards(): sigma_t = jnp.sum(lax.all_to_all(partial, 'row', 0, 0), axis=0)  56.7 us
    ppermute x8, waiting for transfers between devices, gather_col(): up = lax.ppermute(up, 'col', z_shift(cols_count, 1))  42.8 us
    all_to_all x1, blocking collectives, shards(): own = jnp.sum(lax.all_to_all(term, 'row', 0, 0), axis=0)  26.1 us
    ppermute x6, starting transfers between devices, gather_col(): down = lax.ppermute(down, 'col', z_shift(cols_count, -1))  17.7 us
    all_to_all x1, blocking collectives, shards(): pieces = lax.all_to_all(pieces, 'col', 0, 0)  15.7 us
    ppermute x2, starting transfers between devices, gather_col(): other = lax.ppermute(held, 'col', [(i, i ^ 1) for i in range(cols_count)])  12.6 us
    all_to_all x1, blocking collectives, shards(): lax.all_to_all(jnp.broadcast_to(own[None], term.shape), 'row', 0, 0)  10.3 us
    ppermute x1, waiting for transfers between devices, shards(): sigma_t = lax.ppermute(sigma_t, ('row', 'col'), perm)  8.73 us
  transfers between devices with their start and end apart: 17, of which 10 were waited for; matrix products, arithmetic and copies ran while one was open for 6% of the time, Pallas kernels for 0%

profile of v1, /device:TPU:1, one launch (start us, length us, event | category | flops | bytes accessed | tf_op | source)
XLA Modules:
  0.0 241.2 jit_solution(14717554748826874477)
XLA Ops:
  1.9 3.2 %bitcast_dynamic-update-slice_fusion.14 = (f32[8,64,1024]{2,1,0:T(8,128)S(1)}, f32[64,1024]{1,0:T(8,128)S(1)}) fusion(f32[8,64,1024]{2,1,0:T(8,128)S(1)} %broadcast.18.clone, s32[]{:T(128)S(6)} %select_n.140, f32[1024,1024]{1,0:T(8,128)} %param.7, f32[64,1024]{1,0:T(8,128)S(1)} %copy-done.2, f32[1024]{0:T(1024)S(1)} %bitcast.65), kind=kOutput, calls=%fused_computation.27 | convolution fusion | flops 407961600 | bytes 4984836 | tf_op jit(solution)/shard_map/local_scaled/dot_general | solution.py:47
  5.1 2.5 %collective-permute-start = (f32[64,1024]{1,0:T(8,128)S(1)}, f32[64,1024]{1,0:T(8,128)S(1)}, u32[]{:S(2)}, u32[]{:S(2)}) collective-permute-start(f32[64,1024]{1,0:T(8,128)S(1)} %get-tuple-element.7), channel_id=1, source_target_pairs={{0,2},{1,3},{2,4},{3,5},{4,6},{5,7},{6,8},{7,9},{8,10},{9,11},{10,... | collective-permute-start | bytes 786440 | tf_op jit(solution)/shard_map/gather_scaled/ppermute | solution.py:23
  7.7 4.0 %collective-permute-start.1 = (f32[64,1024]{1,0:T(8,128)S(1)}, f32[64,1024]{1,0:T(8,128)S(1)}, u32[]{:S(2)}, u32[]{:S(2)}) collective-permute-start(f32[64,1024]{1,0:T(8,128)S(1)} %get-tuple-element.7), channel_id=1, source_target_pairs={{0,14},{1,15},{2,0},{3,1},{4,2},{5,3},{6,4},{7,5},{8,6},{9,7},{10,... | collective-permute-start | bytes 786440 | tf_op jit(solution)/shard_map/gather_scaled/ppermute | solution.py:26
  11.7 5.9 %collective-permute-done = f32[64,1024]{1,0:T(8,128)S(1)} collective-permute-done((f32[64,1024]{1,0:T(8,128)S(1)}, f32[64,1024]{1,0:T(8,128)S(1)}, u32[]{:S(2)}, u32[]{:S(2)}) %collective-permute-start) | collective-permute-done | bytes 262176 | tf_op jit(solution)/shard_map/gather_scaled/ppermute | solution.py:23
  17.6 2.7 %collective-permute-start.3 = (f32[64,1024]{1,0:T(8,128)S(1)}, f32[64,1024]{1,0:T(8,128)S(1)}, u32[]{:S(2)}, u32[]{:S(2)}) collective-permute-start(f32[64,1024]{1,0:T(8,128)S(1)} %collective-permute-done.1), channel_id=1, source_target_pairs={{0,14},{1,15},{2,0},{3,1},{4,2},{5,3},{6,4},{7,5},{8,6},{9,7},{10,... | collective-permute-start | bytes 786440 | tf_op jit(solution)/shard_map/gather_scaled/ppermute | solution.py:26
  20.4 5.0 %collective-permute-done.2 = f32[64,1024]{1,0:T(8,128)S(1)} collective-permute-done((f32[64,1024]{1,0:T(8,128)S(1)}, f32[64,1024]{1,0:T(8,128)S(1)}, u32[]{:S(2)}, u32[]{:S(2)}) %collective-permute-start.2) | collective-permute-done | bytes 262176 | tf_op jit(solution)/shard_map/gather_scaled/ppermute | solution.py:23
  25.4 2.7 %collective-permute-start.5 = (f32[64,1024]{1,0:T(8,128)S(1)}, f32[64,1024]{1,0:T(8,128)S(1)}, u32[]{:S(2)}, u32[]{:S(2)}) collective-permute-start(f32[64,1024]{1,0:T(8,128)S(1)} %collective-permute-done.3), channel_id=1, source_target_pairs={{0,14},{1,15},{2,0},{3,1},{4,2},{5,3},{6,4},{7,5},{8,6},{9,7},{10,... | collective-permute-start | bytes 786440 | tf_op jit(solution)/shard_map/gather_scaled/ppermute | solution.py:26
  28.1 4.1 %collective-permute-done.4 = f32[64,1024]{1,0:T(8,128)S(1)} collective-permute-done((f32[64,1024]{1,0:T(8,128)S(1)}, f32[64,1024]{1,0:T(8,128)S(1)}, u32[]{:S(2)}, u32[]{:S(2)}) %collective-permute-start.4) | collective-permute-done | bytes 262176 | tf_op jit(solution)/shard_map/gather_scaled/ppermute | solution.py:23
  32.3 6.4 %collective-permute-done.6 = f32[64,1024]{1,0:T(8,128)S(1)} collective-permute-done((f32[64,1024]{1,0:T(8,128)S(1)}, f32[64,1024]{1,0:T(8,128)S(1)}, u32[]{:S(2)}, u32[]{:S(2)}) %collective-permute-start.6) | collective-permute-done | bytes 262176 | tf_op jit(solution)/shard_map/gather_scaled/ppermute | solution.py:23
  38.7 4.5 %collective-permute-start.7 = (f32[8,64,1024]{2,1,0:T(8,128)S(1)}, f32[8,64,1024]{2,1,0:T(8,128)}, u32[]{:S(2)}, u32[]{:S(2)}) collective-permute-start(f32[8,64,1024]{2,1,0:T(8,128)S(1)} %bitcast_dynamic-update-slice_fusion.7), channel_id=1, source_target_pairs={{0,1},{1,0},{2,3},{3,2},{4,5},{5,4},{6,7},{7,6},{8,9},{9,8},{10,11... | collective-permute-start | bytes 6291464 | tf_op jit(solution)/shard_map/gather_scaled/ppermute | solution.py:28
  47.1 2.0 select_bitcast_fusion.3
  49.5 3.4 %copy-done.1 = f32[1024,1024]{1,0:T(8,128)S(1)} copy-done((f32[1024,1024]{1,0:T(8,128)S(1)}, f32[1024,1024]{1,0:T(8,128)}, u32[]{:S(2)}) %copy-start.1) | copy-done | bytes 4194328
  52.9 7.3 %fusion.2 = f32[1024,1024]{1,0:T(8,128)S(1)} fusion(f32[1024,1024]{1,0:T(8,128)S(1)} %bitcast.55, f32[1024,1024]{1,0:T(8,128)S(1)} %copy-done.1, f32[1024,1024]{1,0:T(8,128)S(1)} %bitcast.59), kind=kOutput, calls=%fused_computation.7 | convolution fusion | flops 6444548096 | bytes 16777216 | tf_op jit(solution)/shard_map/product/dot_general | solution.py:58
  60.2 56.7 %all_to_all.22 = f32[16,64,1024]{2,1,0:T(8,128)} all-to-all(f32[16,64,1024]{2,1,0:T(8,128)S(1)} %bitcast.57), channel_id=1, replica_groups=mesh['row'=16,'col'=16] {'row'}, dimensions={0} | all-to-all | bytes 8388608 | tf_op jit(solution)/shard_map/sum_row/all_to_all | solution.py:62
  116.8 2.5 %reduce_sum.18 = f32[64,1024]{1,0:T(8,128)S(1)} reduce(f32[16,64,1024]{2,1,0:T(8,128)} %all_to_all.22, f32[]{:T(128)} %constant.113.clone.1), dimensions={0}, to_apply=%region_0.1 | reduce | flops 983040 | bytes 4456452 | tf_op jit(solution)/shard_map/sum_row/reduce_sum | solution.py:62
  119.3 3.9 %collective-permute-start.8 = (f32[64,1024]{1,0:T(8,128)S(1)}, f32[64,1024]{1,0:T(8,128)S(1)}, u32[]{:S(2)}, u32[]{:S(2)}) collective-permute-start(f32[64,1024]{1,0:T(8,128)S(1)} %reduce_sum.18), channel_id=1, source_target_pairs={{0,0},{1,16},{2,32},{3,48},{4,64},{5,80},{6,96},{7,112},{8,128},{9... | collective-permute-start | bytes 786440 | tf_op jit(solution)/shard_map/transpose_devices/ppermute | solution.py:65
  123.2 4.9 %convert_add_fusion = f32[1024,1024]{1,0:T(8,128)} fusion(f32[1024,1024]{1,0:T(8,128)} %param.7), kind=kLoop, calls=%fused_computation.4 | loop fusion | flops 5242880 | bytes 8388608 | tf_op jit(solution)/shard_map/add | solution.py:41
  129.5 8.7 %collective-permute-done.8 = f32[64,1024]{1,0:T(8,128)S(1)} collective-permute-done((f32[64,1024]{1,0:T(8,128)S(1)}, f32[64,1024]{1,0:T(8,128)S(1)}, u32[]{:S(2)}, u32[]{:S(2)}) %collective-permute-start.8) | collective-permute-done | bytes 262176 | tf_op jit(solution)/shard_map/transpose_devices/ppermute | solution.py:65
  138.3 3.6 %convolution_subtract_fusion = f32[64,1024]{1,0:T(8,128)S(1)} fusion(f32[64,1024]{1,0:T(8,128)S(1)} %fusion.5, f32[64,1024]{1,0:T(8,128)S(1)} %collective-permute-done.8, f32[1024,1024]{1,0:T(8,128)} %bitcast.56), kind=kOutput, calls=%fused_computation.12 | convolution fusion | flops 402718720 | bytes 4980736 | tf_op jit(solution)/shard_map/quad/dot_general | solution.py:67
  142.0 26.1 %all_to_all.23 = f32[16,4,1024]{2,1,0:T(4,128)S(1)} all-to-all(f32[16,4,1024]{2,1,0:T(4,128)S(1)} %reshape.46), channel_id=1, replica_groups=mesh['row'=16,'col'=16] {'row'}, dimensions={0} | all-to-all | bytes 524288 | tf_op jit(solution)/shard_map/sum_diag/all_to_all | solution.py:74
  168.2 10.3 %all_to_all.20 = f32[16,4,1024]{2,1,0:T(4,128)S(1)} all-to-all(f32[16,4,1024]{2,1,0:T(4,128)S(1)} %broadcast_in_dim.79), channel_id=1, replica_groups=mesh['row'=16,'col'=16] {'row'}, dimensions={0} | all-to-all | bytes 524288 | tf_op jit(solution)/shard_map/sum_diag/all_to_all | solution.py:75
  178.6 2.7 %collective-permute-start.10 = (f32[64,1024]{1,0:T(8,128)S(1)}, f32[64,1024]{1,0:T(8,128)S(1)}, u32[]{:S(2)}, u32[]{:S(2)}) collective-permute-start(f32[64,1024]{1,0:T(8,128)S(1)} %reshape.48), channel_id=1, source_target_pairs={{0,14},{1,15},{2,0},{3,1},{4,2},{5,3},{6,4},{7,5},{8,6},{9,7},{10,... | collective-permute-start | bytes 786440 | tf_op jit(solution)/shard_map/sum_diag/ppermute | solution.py:26
  181.7 3.4 %collective-permute-done.9 = f32[64,1024]{1,0:T(8,128)S(1)} collective-permute-done((f32[64,1024]{1,0:T(8,128)S(1)}, f32[64,1024]{1,0:T(8,128)S(1)}, u32[]{:S(2)}, u32[]{:S(2)}) %collective-permute-start.9) | collective-permute-done | bytes 262176 | tf_op jit(solution)/shard_map/sum_diag/ppermute | solution.py:23
  185.1 2.7 %collective-permute-start.12 = (f32[64,1024]{1,0:T(8,128)S(1)}, f32[64,1024]{1,0:T(8,128)S(1)}, u32[]{:S(2)}, u32[]{:S(2)}) collective-permute-start(f32[64,1024]{1,0:T(8,128)S(1)} %collective-permute-done.10), channel_id=1, source_target_pairs={{0,14},{1,15},{2,0},{3,1},{4,2},{5,3},{6,4},{7,5},{8,6},{9,7},{10,... | collective-permute-start | bytes 786440 | tf_op jit(solution)/shard_map/sum_diag/ppermute | solution.py:26
  187.9 4.0 %collective-permute-done.11 = f32[64,1024]{1,0:T(8,128)S(1)} collective-permute-done((f32[64,1024]{1,0:T(8,128)S(1)}, f32[64,1024]{1,0:T(8,128)S(1)}, u32[]{:S(2)}, u32[]{:S(2)}) %collective-permute-start.11) | collective-permute-done | bytes 262176 | tf_op jit(solution)/shard_map/sum_diag/ppermute | solution.py:23
  191.9 2.9 %collective-permute-start.14 = (f32[64,1024]{1,0:T(8,128)S(1)}, f32[64,1024]{1,0:T(8,128)S(1)}, u32[]{:S(2)}, u32[]{:S(2)}) collective-permute-start(f32[64,1024]{1,0:T(8,128)S(1)} %collective-permute-done.12), channel_id=1, source_target_pairs={{0,14},{1,15},{2,0},{3,1},{4,2},{5,3},{6,4},{7,5},{8,6},{9,7},{10,... | collective-permute-start | bytes 786440 | tf_op jit(solution)/shard_map/sum_diag/ppermute | solution.py:26
  194.9 4.9 %collective-permute-done.13 = f32[64,1024]{1,0:T(8,128)S(1)} collective-permute-done((f32[64,1024]{1,0:T(8,128)S(1)}, f32[64,1024]{1,0:T(8,128)S(1)}, u32[]{:S(2)}, u32[]{:S(2)}) %collective-permute-start.13) | collective-permute-done | bytes 262176 | tf_op jit(solution)/shard_map/sum_diag/ppermute | solution.py:23
  199.9 9.0 %collective-permute-done.15 = f32[64,1024]{1,0:T(8,128)S(1)} collective-permute-done((f32[64,1024]{1,0:T(8,128)S(1)}, f32[64,1024]{1,0:T(8,128)S(1)}, u32[]{:S(2)}, u32[]{:S(2)}) %collective-permute-start.15) | collective-permute-done | bytes 262176 | tf_op jit(solution)/shard_map/sum_diag/ppermute | solution.py:23
  208.9 8.1 %collective-permute-start.16 = (f32[8,64,1024]{2,1,0:T(8,128)S(1)}, f32[8,64,1024]{2,1,0:T(8,128)}, u32[]{:S(2)}, u32[]{:S(2)}) collective-permute-start(f32[8,64,1024]{2,1,0:T(8,128)S(1)} %bitcast_dynamic-update-slice_fusion), channel_id=1, source_target_pairs={{0,1},{1,0},{2,3},{3,2},{4,5},{5,4},{6,7},{7,6},{8,9},{9,8},{10,11... | collective-permute-start | bytes 6291464 | tf_op jit(solution)/shard_map/sum_diag/ppermute | solution.py:28
  217.6 15.7 %all_to_all.21 = f32[16,1,4096]{2,1,0:T(1,128)S(1)} all-to-all(f32[16,1,4096]{2,1,0:T(1,128)S(1)} %reshape.51), channel_id=1, replica_groups=mesh['row'=16,'col'=16] {'col'}, dimensions={0} | all-to-all | bytes 524288 | tf_op jit(solution)/shard_map/sigma_out/all_to_all | solution.py:79
  236.3 2.0 select_bitcast_fusion.1
  238.9 2.3 copy.15
  (59 shorter events, 12.0 us)
Async XLA Ops:
  0.6 1.3 copy-start.2
  5.1 12.5 %collective-permute-start = (f32[64,1024]{1,0:T(8,128)S(1)}, f32[64,1024]{1,0:T(8,128)S(1)}, u32[]{:S(2)}, u32[]{:S(2)}) collective-permute-start(f32[64,1024]{1,0:T(8,128)S(1)} %get-tuple-element.7), channel_id=1, source_target_pairs={{0,2},{1,3},{2,4},{3,5},{4,6},{5,7},{6,8},{7,9},{8,10},{9,11},{10,... | collective-permute-start | bytes 786440 | tf_op jit(solution)/shard_map/gather_scaled/ppermute | solution.py:23
  7.7 10.0 %collective-permute-start.1 = (f32[64,1024]{1,0:T(8,128)S(1)}, f32[64,1024]{1,0:T(8,128)S(1)}, u32[]{:S(2)}, u32[]{:S(2)}) collective-permute-start(f32[64,1024]{1,0:T(8,128)S(1)} %get-tuple-element.7), channel_id=1, source_target_pairs={{0,14},{1,15},{2,0},{3,1},{4,2},{5,3},{6,4},{7,5},{8,6},{9,7},{10,... | collective-permute-start | bytes 786440 | tf_op jit(solution)/shard_map/gather_scaled/ppermute | solution.py:26
  17.6 7.8 %collective-permute-start.2 = (f32[64,1024]{1,0:T(8,128)S(1)}, f32[64,1024]{1,0:T(8,128)S(1)}, u32[]{:S(2)}, u32[]{:S(2)}) collective-permute-start(f32[64,1024]{1,0:T(8,128)S(1)} %collective-permute-done), channel_id=1, source_target_pairs={{0,2},{1,3},{2,4},{3,5},{4,6},{5,7},{6,8},{7,9},{8,10},{9,11},{10,... | collective-permute-start | bytes 786440 | tf_op jit(solution)/shard_map/gather_scaled/ppermute | solution.py:23
  17.6 7.8 %collective-permute-start.3 = (f32[64,1024]{1,0:T(8,128)S(1)}, f32[64,1024]{1,0:T(8,128)S(1)}, u32[]{:S(2)}, u32[]{:S(2)}) collective-permute-start(f32[64,1024]{1,0:T(8,128)S(1)} %collective-permute-done.1), channel_id=1, source_target_pairs={{0,14},{1,15},{2,0},{3,1},{4,2},{5,3},{6,4},{7,5},{8,6},{9,7},{10,... | collective-permute-start | bytes 786440 | tf_op jit(solution)/shard_map/gather_scaled/ppermute | solution.py:26
  25.4 6.9 %collective-permute-start.4 = (f32[64,1024]{1,0:T(8,128)S(1)}, f32[64,1024]{1,0:T(8,128)S(1)}, u32[]{:S(2)}, u32[]{:S(2)}) collective-permute-start(f32[64,1024]{1,0:T(8,128)S(1)} %collective-permute-done.2), channel_id=1, source_target_pairs={{0,2},{1,3},{2,4},{3,5},{4,6},{5,7},{6,8},{7,9},{8,10},{9,11},{10,... | collective-permute-start | bytes 786440 | tf_op jit(solution)/shard_map/gather_scaled/ppermute | solution.py:23
  25.4 6.9 %collective-permute-start.5 = (f32[64,1024]{1,0:T(8,128)S(1)}, f32[64,1024]{1,0:T(8,128)S(1)}, u32[]{:S(2)}, u32[]{:S(2)}) collective-permute-start(f32[64,1024]{1,0:T(8,128)S(1)} %collective-permute-done.3), channel_id=1, source_target_pairs={{0,14},{1,15},{2,0},{3,1},{4,2},{5,3},{6,4},{7,5},{8,6},{9,7},{10,... | collective-permute-start | bytes 786440 | tf_op jit(solution)/shard_map/gather_scaled/ppermute | solution.py:26
  32.3 6.4 %collective-permute-start.6 = (f32[64,1024]{1,0:T(8,128)S(1)}, f32[64,1024]{1,0:T(8,128)S(1)}, u32[]{:S(2)}, u32[]{:S(2)}) collective-permute-start(f32[64,1024]{1,0:T(8,128)S(1)} %collective-permute-done.4), channel_id=1, source_target_pairs={{0,2},{1,3},{2,4},{3,5},{4,6},{5,7},{6,8},{7,9},{8,10},{9,11},{10,... | collective-permute-start | bytes 786440 | tf_op jit(solution)/shard_map/gather_scaled/ppermute | solution.py:23
  38.7 8.4 %collective-permute-start.7 = (f32[8,64,1024]{2,1,0:T(8,128)S(1)}, f32[8,64,1024]{2,1,0:T(8,128)}, u32[]{:S(2)}, u32[]{:S(2)}) collective-permute-start(f32[8,64,1024]{2,1,0:T(8,128)S(1)} %bitcast_dynamic-update-slice_fusion.7), channel_id=1, source_target_pairs={{0,1},{1,0},{2,3},{3,2},{4,5},{5,4},{6,7},{7,6},{8,9},{9,8},{10,11... | collective-permute-start | bytes 6291464 | tf_op jit(solution)/shard_map/gather_scaled/ppermute | solution.py:28
  49.2 3.7 %copy-start.1 = (f32[1024,1024]{1,0:T(8,128)S(1)}, f32[1024,1024]{1,0:T(8,128)}, u32[]{:S(2)}) copy-start(f32[1024,1024]{1,0:T(8,128)} %param.5) | copy-start | bytes 12582916
  49.5 10.7 %copy-start = (f32[8,2,64,1024]{3,2,1,0:T(8,128)}, f32[8,2,64,1024]{3,2,1,0:T(8,128)S(1)}, u32[]{:S(2)}) copy-start(f32[8,2,64,1024]{3,2,1,0:T(8,128)S(1)} %pad_maximum_fusion) | copy-start | bytes 12582916
  119.3 18.9 %collective-permute-start.8 = (f32[64,1024]{1,0:T(8,128)S(1)}, f32[64,1024]{1,0:T(8,128)S(1)}, u32[]{:S(2)}, u32[]{:S(2)}) collective-permute-start(f32[64,1024]{1,0:T(8,128)S(1)} %reduce_sum.18), channel_id=1, source_target_pairs={{0,0},{1,16},{2,32},{3,48},{4,64},{5,80},{6,96},{7,112},{8,128},{9... | collective-permute-start | bytes 786440 | tf_op jit(solution)/shard_map/transpose_devices/ppermute | solution.py:65
  178.5 6.5 %collective-permute-start.9 = (f32[64,1024]{1,0:T(8,128)S(1)}, f32[64,1024]{1,0:T(8,128)S(1)}, u32[]{:S(2)}, u32[]{:S(2)}) collective-permute-start(f32[64,1024]{1,0:T(8,128)S(1)} %reshape.48), channel_id=1, source_target_pairs={{0,2},{1,3},{2,4},{3,5},{4,6},{5,7},{6,8},{7,9},{8,10},{9,11},{10,... | collective-permute-start | bytes 786440 | tf_op jit(solution)/shard_map/sum_diag/ppermute | solution.py:23
  178.6 6.5 %collective-permute-start.10 = (f32[64,1024]{1,0:T(8,128)S(1)}, f32[64,1024]{1,0:T(8,128)S(1)}, u32[]{:S(2)}, u32[]{:S(2)}) collective-permute-start(f32[64,1024]{1,0:T(8,128)S(1)} %reshape.48), channel_id=1, source_target_pairs={{0,14},{1,15},{2,0},{3,1},{4,2},{5,3},{6,4},{7,5},{8,6},{9,7},{10,... | collective-permute-start | bytes 786440 | tf_op jit(solution)/shard_map/sum_diag/ppermute | solution.py:26
  185.0 6.8 %collective-permute-start.11 = (f32[64,1024]{1,0:T(8,128)S(1)}, f32[64,1024]{1,0:T(8,128)S(1)}, u32[]{:S(2)}, u32[]{:S(2)}) collective-permute-start(f32[64,1024]{1,0:T(8,128)S(1)} %collective-permute-done.9), channel_id=1, source_target_pairs={{0,2},{1,3},{2,4},{3,5},{4,6},{5,7},{6,8},{7,9},{8,10},{9,11},{10,... | collective-permute-start | bytes 786440 | tf_op jit(solution)/shard_map/sum_diag/ppermute | solution.py:23
  185.1 6.8 %collective-permute-start.12 = (f32[64,1024]{1,0:T(8,128)S(1)}, f32[64,1024]{1,0:T(8,128)S(1)}, u32[]{:S(2)}, u32[]{:S(2)}) collective-permute-start(f32[64,1024]{1,0:T(8,128)S(1)} %collective-permute-done.10), channel_id=1, source_target_pairs={{0,14},{1,15},{2,0},{3,1},{4,2},{5,3},{6,4},{7,5},{8,6},{9,7},{10,... | collective-permute-start | bytes 786440 | tf_op jit(solution)/shard_map/sum_diag/ppermute | solution.py:26
  191.9 7.9 %collective-permute-start.13 = (f32[64,1024]{1,0:T(8,128)S(1)}, f32[64,1024]{1,0:T(8,128)S(1)}, u32[]{:S(2)}, u32[]{:S(2)}) collective-permute-start(f32[64,1024]{1,0:T(8,128)S(1)} %collective-permute-done.11), channel_id=1, source_target_pairs={{0,2},{1,3},{2,4},{3,5},{4,6},{5,7},{6,8},{7,9},{8,10},{9,11},{10,... | collective-permute-start | bytes 786440 | tf_op jit(solution)/shard_map/sum_diag/ppermute | solution.py:23
  191.9 7.9 %collective-permute-start.14 = (f32[64,1024]{1,0:T(8,128)S(1)}, f32[64,1024]{1,0:T(8,128)S(1)}, u32[]{:S(2)}, u32[]{:S(2)}) collective-permute-start(f32[64,1024]{1,0:T(8,128)S(1)} %collective-permute-done.12), channel_id=1, source_target_pairs={{0,14},{1,15},{2,0},{3,1},{4,2},{5,3},{6,4},{7,5},{8,6},{9,7},{10,... | collective-permute-start | bytes 786440 | tf_op jit(solution)/shard_map/sum_diag/ppermute | solution.py:26
  199.8 9.1 %collective-permute-start.15 = (f32[64,1024]{1,0:T(8,128)S(1)}, f32[64,1024]{1,0:T(8,128)S(1)}, u32[]{:S(2)}, u32[]{:S(2)}) collective-permute-start(f32[64,1024]{1,0:T(8,128)S(1)} %collective-permute-done.13), channel_id=1, source_target_pairs={{0,2},{1,3},{2,4},{3,5},{4,6},{5,7},{6,8},{7,9},{8,10},{9,11},{10,... | collective-permute-start | bytes 786440 | tf_op jit(solution)/shard_map/sum_diag/ppermute | solution.py:23
  208.9 27.4 %collective-permute-start.16 = (f32[8,64,1024]{2,1,0:T(8,128)S(1)}, f32[8,64,1024]{2,1,0:T(8,128)}, u32[]{:S(2)}, u32[]{:S(2)}) collective-permute-start(f32[8,64,1024]{2,1,0:T(8,128)S(1)} %bitcast_dynamic-update-slice_fusion), channel_id=1, source_target_pairs={{0,1},{1,0},{2,3},{3,2},{4,5},{5,4},{6,7},{7,6},{8,9},{9,8},{10,11... | collective-permute-start | bytes 6291464 | tf_op jit(solution)/shard_map/sum_diag/ppermute | solution.py:28
